TPU v7x, 32 devices: a whole 2x2x4 slice. The times are simulated.
32 devices in a mesh: dom: 8 (over y, x, core), band: 4 (over z).
Axes of the slice: x: 2, y: 2, z: 4, core: 2. Of those that a mesh axis runs over, the one named last changes fastest.
Arguments:
- psi: float32 [512, 48, 512], P('band', 'dom'), may hold values from -40 to 40, as said below
- potential: float32 [48, 512], P('dom'), may hold values from -3 to 1
Outputs:
- filtered_basis: float32 [512, 48, 512], P('band', 'dom')
Inputs may be any that keep to these rules, and one draw needn't show every extreme that they name: `psi`: real-valued band functions.
All inputs are finite; a program needn't handle non-finite values.
Results may differ from a plain program's by a relative error of at most 0.0002.
Values sent between devices are 32-bit elements; how exact they have to be, the bound alone decides.
A program may use at most 128 MiB of HBM per device.

v0:
```python
import jax
import jax.numpy as jnp
from jax import lax
from jax.sharding import PartitionSpec as P

LX = 32
DEG = 4


COEF = (
    -5369.0 / 1800.0,
    12.0 / 7.0,
    -15.0 / 56.0,
    10.0 / 189.0,
    -1.0 / 112.0,
    2.0 / 1925.0,
    -1.0 / 16632.0,
)
INV_SPACING2 = 4.0
CENTRE = 24.0
HALF_WIDTH = 20.0


def with_halo(block, sides, width):
    for axis, dim in sides:
        count = lax.axis_size(axis)
        forward = [(i, i + 1) for i in range(count - 1)]
        backward = [(target, source) for source, target in forward]
        low = lax.ppermute(
            lax.slice_in_dim(block, block.shape[dim] - width, None, axis=dim), axis, forward
        )
        high = lax.ppermute(lax.slice_in_dim(block, 0, width, axis=dim), axis, backward)
        block = jnp.concatenate([low, block, high], axis=dim)
    return block


def shift_x(values, step):
    amount = step % LX
    column = lax.broadcasted_iota(jnp.int32, values.shape, 2) % LX
    return jnp.where(
        column >= amount, jnp.roll(values, amount, 2), jnp.roll(values, amount - LX, 2)
    )


def shift_y(values, step):
    return jnp.roll(values, step * LX, 2)


def hamiltonian(values, potential):
    depth = values.shape[1]
    padded = with_halo(values, (("dom", 1),), 6)
    summed = 3.0 * COEF[0] * values
    for step in range(1, 7):
        beside_all = shift_x(values, step) + shift_x(values, -step)
        beside_all = beside_all + shift_y(values, step) + shift_y(values, -step)
        beside_all = (
            beside_all
            + padded[:, 6 + step : 6 + step + depth]
            + padded[:, 6 - step : 6 - step + depth]
        )
        summed = summed + COEF[step] * beside_all
    return -0.5 * INV_SPACING2 * summed + potential[None] * values


def chebyshev(start, potential):
    previous = start
    current = (hamiltonian(start, potential) - CENTRE * start) / HALF_WIDTH
    for degree in range(1, DEG):
        following = (
            2.0 * (hamiltonian(current, potential) - CENTRE * current) / HALF_WIDTH - previous
        )
        previous, current = (current, following)
    return current


def shards(psi, potential):
    filtered = chebyshev(psi, potential)
    tile_bands = psi.shape[0]
    points_dev = psi.shape[1] * psi.shape[2]
    all_points = points_dev * lax.axis_size("dom")
    flatrows = filtered.reshape(tile_bands, points_dev)
    spread = lax.all_to_all(flatrows, "band", split_axis=1, concat_axis=0, tiled=True)
    partial_gram = jnp.dot(
        spread, spread.T, precision=lax.Precision.HIGHEST, preferred_element_type=jnp.float32
    )
    gram = lax.psum(partial_gram, ("dom", "band")) / all_points
    lower = jnp.linalg.cholesky(gram)
    solved = lax.linalg.triangular_solve(lower, spread, left_side=True, lower=True)
    rotated = lax.all_to_all(solved, "band", split_axis=0, concat_axis=1, tiled=True)
    return rotated.reshape(psi.shape)


def solution(mesh):
    placed = (P("band", "dom", None), P("dom", None))
    return jax.shard_map(
        shards, mesh=mesh, in_specs=placed, out_specs=P("band", "dom", None), check_vma=False
    )
```

profile of v0, /device:TPU:25, one launch (start us, length us, event | category | flops | bytes accessed | tf_op | source)
XLA Modules:
  0.0 764.2 jit_solution(13362882973609732826)
XLA Ops:
  11.0 3.0 collective-permute-start.1
  63.4 31.0 %broadcast_multiply_fusion = (f32[128,6,512]{0,2,1:T(8,128)S(1)}, f32[128,6,512]{0,2,1:T(8,128)}) fusion(f32[128,6,512]{0,2,1:T(8,128)S(1)} %copy.5, f32[6,512]{1,0:T(8,128)S(1)} %copy-done.11, f32[128,6,512]{0,2,1:T(8,128)} %copy-done.4, f32[128,6,512]{0,2,1:T(8,128)} %copy-done.3, f32[128,6,192]{0,2,1:T(8,128)} %get-tuple-element.310, ...), kind=kLoop, calls=%fused_computation.373 | loop fusion | flops 47185920 | bytes 64504320 | tf_op jit(solution)/shard_map/div | solution.py:67
  121.0 3.6 collective-permute-start.3
  145.3 7.7 %collective-permute-done.2 = f32[128,6,512]{0,2,1:T(8,128)S(1)} collective-permute-done((f32[128,6,512]{0,2,1:T(8,128)S(1)}, f32[128,6,512]{0,2,1:T(8,128)S(1)}, u32[]{:S(2)}, u32[]{:S(2)}) %collective-permute-start.2) | collective-permute-done | bytes 1572896 | tf_op jit(solution)/shard_map/ppermute | solution.py:32
  154.7 35.4 %fusion.69 = f32[128,6,512]{0,2,1:T(8,128)S(1)} fusion(f32[128,6,512]{0,2,1:T(8,128)S(1)} %copy.5, f32[128,6,512]{0,2,1:T(8,128)} %copy-done.8, f32[128,6,512]{0,2,1:T(8,128)} %copy-done.6, f32[128,6,512]{0,2,1:T(8,128)} %copy-done, f32[128,6,511]{0,2,1:T(8,128)} %get-tuple-element.234, f32[128,6,1]{0,2,1:T(1,128)} %get-tuple-element.236, ...), kind=kLoop, calls=%fused_computation.147 | loop fusion | flops 47579136 | bytes 66077184 | tf_op jit(solution)/shard_map/sub | solution.py:70
  216.5 3.6 collective-permute-start.5
  241.0 3.0 collective-permute-done.4
  245.7 33.4 %fusion.81 = f32[128,6,512]{0,2,1:T(8,128)S(1)} fusion(f32[128,6,512]{0,2,1:T(8,128)} %copy-done.10, f32[128,6,512]{0,2,1:T(8,128)} %copy-done.9, f32[128,6,512]{0,2,1:T(8,128)S(1)} %fusion.69, f32[128,6,511]{0,2,1:T(8,128)} %get-tuple-element.162, f32[128,6,1]{0,2,1:T(1,128)} %get-tuple-element.164, f32[128,6,31]{0,2,1:T(8,128)} %get-tuple-element.166, ...), kind=kLoop, calls=%fused_computation.159 | loop fusion | flops 47972352 | bytes 64504320 | tf_op jit(solution)/shard_map/sub | solution.py:70
  305.7 4.1 collective-permute-start.7
  332.7 33.2 %fusion.93 = f32[128,6,512]{0,2,1:T(8,128)} fusion(f32[128,6,512]{0,2,1:T(8,128)S(1)} %fusion.69, f32[128,6,512]{0,2,1:T(8,128)} %copy-done.7, f32[128,6,512]{0,2,1:T(8,128)} %copy-done.5, f32[128,6,512]{0,2,1:T(8,128)S(1)} %fusion.81, f32[128,6,511]{0,2,1:T(8,128)} %get-tuple-element.90, f32[128,6,1]{0,2,1:T(1,128)} %get-tuple-element.92, ...), kind=kLoop, calls=%fused_computation.171 | loop fusion | flops 47579136 | bytes 64504320 | tf_op jit(solution)/shard_map/sub | solution.py:70
  366.0 38.6 %all_to_all.35 = f32[128,4,768]{0,2,1:T(8,128)S(1)} all-to-all(f32[128,4,768]{0,2,1:T(8,128)} %bitcast.80), channel_id=1, replica_groups=mesh['dom'=8,'band'=4] {'band'}, dimensions={1} | all-to-all | bytes 3145728 | tf_op jit(solution)/shard_map/all_to_all | solution.py:82
  405.1 3.6 fusion.445
  408.8 151.9 %all-reduce.3.cloned.1.call-done = f32[512,512]{0,1:T(8,128)} async-done(((f32[512,512]{0,1:T(8,128)}), f32[512,512]{0,1:T(8,128)}) %all-reduce.3.cloned.1.call-update) | async-done | bytes 1048592 | tf_op jit(solution)/shard_map/psum | solution.py:86
  568.1 11.7 %cholesky.104 = f32[128,128]{1,0:T(8,128)S(1)} custom-call(f32[128,128]{1,0:T(8,128)S(1)} %cholesky.266), custom_call_target="Cholesky" | custom-call | tf_op jit(solution)/shard_map/jit(cholesky)/cholesky | solution.py:87
  580.0 9.8 %custom-call.30 = f32[1,128,128]{1,2,0:T(8,128)S(1)} custom-call(f32[1,128,128]{2,1,0:T(8,128)S(1)} %get-tuple-element.322), custom_call_target="InvertDiagBlocksLowerTriangular" | custom-call | tf_op jit(solution)/shard_map/jit(cholesky)/cholesky | solution.py:87
  592.3 11.9 %cholesky.217 = f32[128,128]{1,0:T(8,128)S(1)} custom-call(f32[128,128]{1,0:T(8,128)S(1)} %cholesky.270), custom_call_target="Cholesky" | custom-call | tf_op jit(solution)/shard_map/jit(cholesky)/cholesky | solution.py:87
  604.2 9.8 %custom-call.31 = f32[1,128,128]{1,2,0:T(8,128)S(1)} custom-call(f32[1,128,128]{2,1,0:T(8,128)S(1)} %get-tuple-element.319), custom_call_target="InvertDiagBlocksLowerTriangular" | custom-call | tf_op jit(solution)/shard_map/jit(cholesky)/cholesky | solution.py:87
  615.6 11.7 %cholesky.238 = f32[128,128]{1,0:T(8,128)S(1)} custom-call(f32[128,128]{1,0:T(8,128)S(1)} %cholesky.275), custom_call_target="Cholesky" | custom-call | tf_op jit(solution)/shard_map/jit(cholesky)/cholesky | solution.py:87
  628.1 9.8 %custom-call.32 = f32[1,128,128]{1,2,0:T(8,128)S(1)} custom-call(f32[1,128,128]{2,1,0:T(8,128)S(1)} %get-tuple-element.316), custom_call_target="InvertDiagBlocksLowerTriangular" | custom-call | tf_op jit(solution)/shard_map/jit(cholesky)/cholesky | solution.py:87
  639.3 11.9 %cholesky.255 = f32[128,128]{1,0:T(8,128)S(1)} custom-call(f32[128,128]{1,0:T(8,128)S(1)} %convolution_subtract_fusion.5), custom_call_target="Cholesky" | custom-call | tf_op jit(solution)/shard_map/jit(cholesky)/cholesky | solution.py:87
  656.3 11.6 %while.1 = (s32[]{:T(128)}, f32[512,512]{1,0:T(8,128)}, s32[4,2]{0,1:T(2,128)S(1)}, f32[4,128,128]{2,1,0:T(8,128)S(1)}, s32[]{:T(128)}) while((s32[]{:T(128)}, f32[512,512]{1,0:T(8,128)}, s32[4,2]{0,1:T(2,128)S(1)}, f32[4,128,128]{2,1,0:T(8,128)S(1)}, s32[]{:T(128)}) %tuple.172), condition=%wide.while_cond, body=%wide.while_body.sunk | while | flops 2 | bytes 131181 | solution.py:88
  667.9 39.3 %custom-call.33 = f32[4,128,128]{1,2,0:T(8,128)S(1)} custom-call(f32[4,128,128]{2,1,0:T(8,128)S(1)} %get-tuple-element.12), custom_call_target="InvertDiagBlocksLowerTriangular" | custom-call | tf_op jit(solution)/shard_map/triangular_solve | solution.py:88
  712.8 3.0 convolution_subtract_fusion
  716.9 38.6 %all_to_all.36 = f32[4,128,768]{1,2,0:T(8,128)S(1)} all-to-all(f32[4,128,768]{1,2,0:T(8,128)S(1)} %copy.88), channel_id=1, replica_groups=mesh['dom'=8,'band'=4] {'band'}, dimensions={0} | all-to-all | bytes 3145728 | tf_op jit(solution)/shard_map/all_to_all | solution.py:89
  (231 shorter events, 237.5 us)
Async XLA Ops:
  6.5 554.2 %all-reduce.3.cloned.1.call-start = ((), (), s32[]{:S(2)}) async-start(), calls=%async_computation.2 | async-start | bytes 2097152 | tf_op jit(solution)/shard_map/psum | solution.py:86
  8.4 53.3 %collective-permute-start = (f32[128,6,512]{0,2,1:T(8,128)S(1)}, f32[128,6,512]{0,2,1:T(8,128)S(1)}, u32[]{:S(2)}, u32[]{:S(2)}) collective-permute-start(f32[128,6,512]{0,2,1:T(8,128)S(1)} %copy.5), channel_id=1, source_target_pairs={{4,0},{8,4},{12,8},{16,12},{20,16},{24,20},{28,24},{5,1},{9,5},{13... | collective-permute-start | bytes 4718600 | tf_op jit(solution)/shard_map/ppermute | solution.py:32
  11.0 50.7 %collective-permute-start.1 = (f32[128,6,512]{0,2,1:T(8,128)S(1)}, f32[128,6,512]{0,2,1:T(8,128)S(1)}, u32[]{:S(2)}, u32[]{:S(2)}) collective-permute-start(f32[128,6,512]{0,2,1:T(8,128)S(1)} %copy.5), channel_id=1, source_target_pairs={{0,4},{4,8},{8,12},{12,16},{16,20},{20,24},{24,28},{1,5},{5,9},{9,... | collective-permute-start | bytes 4718600 | tf_op jit(solution)/shard_map/ppermute | solution.py:29
  43.2 9.7 %copy-start.11 = (f32[6,512]{1,0:T(8,128)S(1)}, f32[6,512]{1,0:T(8,128)}, u32[]{:S(2)}) copy-start(f32[6,512]{1,0:T(8,128)} %param.3) | copy-start | bytes 36868
  61.7 1.1 copy-start.3
  61.8 1.7 copy-start.4
  94.4 48.9 %copy-start = (f32[128,6,512]{0,2,1:T(8,128)}, f32[128,6,512]{0,2,1:T(8,128)S(1)}, u32[]{:S(2)}) copy-start(f32[128,6,512]{0,2,1:T(8,128)S(1)} %get-tuple-element.21) | copy-start | bytes 4718596
  119.1 33.9 %collective-permute-start.2 = (f32[128,6,512]{0,2,1:T(8,128)S(1)}, f32[128,6,512]{0,2,1:T(8,128)S(1)}, u32[]{:S(2)}, u32[]{:S(2)}) collective-permute-start(f32[128,6,512]{0,2,1:T(8,128)S(1)} %get-tuple-element.21), channel_id=1, source_target_pairs={{4,0},{8,4},{12,8},{16,12},{20,16},{24,20},{28,24},{5,1},{9,5},{13... | collective-permute-start | bytes 4718600 | tf_op jit(solution)/shard_map/ppermute | solution.py:32
  121.0 32.0 %collective-permute-start.3 = (f32[128,6,512]{0,2,1:T(8,128)S(1)}, f32[128,6,512]{0,2,1:T(8,128)S(1)}, u32[]{:S(2)}, u32[]{:S(2)}) collective-permute-start(f32[128,6,512]{0,2,1:T(8,128)S(1)} %get-tuple-element.21), channel_id=1, source_target_pairs={{0,4},{4,8},{8,12},{12,16},{16,20},{20,24},{24,28},{1,5},{5,9},{9,... | collective-permute-start | bytes 4718600 | tf_op jit(solution)/shard_map/ppermute | solution.py:29
  153.0 1.2 copy-start.6
  153.0 1.7 copy-start.8
  214.6 29.4 %collective-permute-start.4 = (f32[128,6,512]{0,2,1:T(8,128)S(1)}, f32[128,6,512]{0,2,1:T(8,128)S(1)}, u32[]{:S(2)}, u32[]{:S(2)}) collective-permute-start(f32[128,6,512]{0,2,1:T(8,128)S(1)} %fusion.69), channel_id=1, source_target_pairs={{4,0},{8,4},{12,8},{16,12},{20,16},{24,20},{28,24},{5,1},{9,5},{13... | collective-permute-start | bytes 4718600 | tf_op jit(solution)/shard_map/ppermute | solution.py:32
  216.5 27.5 %collective-permute-start.5 = (f32[128,6,512]{0,2,1:T(8,128)S(1)}, f32[128,6,512]{0,2,1:T(8,128)S(1)}, u32[]{:S(2)}, u32[]{:S(2)}) collective-permute-start(f32[128,6,512]{0,2,1:T(8,128)S(1)} %fusion.69), channel_id=1, source_target_pairs={{0,4},{4,8},{8,12},{12,16},{16,20},{20,24},{24,28},{1,5},{5,9},{9,... | collective-permute-start | bytes 4718600 | tf_op jit(solution)/shard_map/ppermute | solution.py:29
  244.1 1.2 copy-start.9
  244.1 1.7 copy-start.10
  303.8 26.7 %collective-permute-start.6 = (f32[128,6,512]{0,2,1:T(8,128)S(1)}, f32[128,6,512]{0,2,1:T(8,128)S(1)}, u32[]{:S(2)}, u32[]{:S(2)}) collective-permute-start(f32[128,6,512]{0,2,1:T(8,128)S(1)} %fusion.81), channel_id=1, source_target_pairs={{4,0},{8,4},{12,8},{16,12},{20,16},{24,20},{28,24},{5,1},{9,5},{13... | collective-permute-start | bytes 4718600 | tf_op jit(solution)/shard_map/ppermute | solution.py:32
  305.7 24.8 %collective-permute-start.7 = (f32[128,6,512]{0,2,1:T(8,128)S(1)}, f32[128,6,512]{0,2,1:T(8,128)S(1)}, u32[]{:S(2)}, u32[]{:S(2)}) collective-permute-start(f32[128,6,512]{0,2,1:T(8,128)S(1)} %fusion.81), channel_id=1, source_target_pairs={{0,4},{4,8},{8,12},{12,16},{16,20},{20,24},{24,28},{1,5},{5,9},{9,... | collective-permute-start | bytes 4718600 | tf_op jit(solution)/shard_map/ppermute | solution.py:29
  330.5 1.1 copy-start.5
  331.6 1.1 copy-start.7
  563.0 2.6 copy-start.1
  567.1 1.0 copy-start.2
Sparse Core Ops, SparseCore 0:
  408.9 151.7 all-reduce.2
where the time goes:
time: 774 us; the launch traced here: 764 us
  other arithmetic  259 us (33%)
  local copies, waits for them, and re-layouts  208 us (27%)
  waiting for transfers between devices  163 us (21%)
  blocking collectives  77.3 us (10%)
  starting transfers between devices  22.7 us (3%)
  matrix products  18.2 us (2%)
  between operations  16.6 us (2%)
    psum x1, waiting for transfers between devices, shards(): gram = lax.psum(partial_gram, ('dom', 'band')) / all_points  152 us
    sub x3, other arithmetic, chebyshev(): 2.0 * (hamiltonian(current, potential) - CENTRE * current) / HALF_WIDTH  102 us
    another operation x14, other arithmetic, shards(): lower = jnp.linalg.cholesky(gram)  78.8 us
    slice x48, local copies, waits for them, and re-layouts, shift_y(): return jnp.roll(values, step * LX, 2)  60.8 us
    slice x48, local copies, waits for them, and re-layouts, shift_x(): jnp.roll(values, amount - LX, 2)  60.4 us
    slice x48, local copies, waits for them, and re-layouts, shift_x(): jnp.roll(values, amount, 2)  60 us
    another operation x4, other arithmetic, shards(): lax.linalg.triangular_solve(lower, spread, left_side=True, lower=True)  40.5 us
    all_to_all x1, blocking collectives, shards(): lax.all_to_all(flatrows, 'band', split_axis=1, concat_axis=0, tiled=True)  38.6 us
  transfers between devices with their start and end apart: 9, of which 3 were waited for; matrix products, arithmetic and copies ran while one was open for 14% of the time, Pallas kernels for 0%

commit v1 on v0

v1 whole, which is shorter than its diff:
```python
import functools

import jax
import jax.numpy as jnp
import numpy as np
from jax import lax
from jax.experimental import pallas as pl
from jax.experimental.pallas import tpu as pltpu
from jax.sharding import PartitionSpec as P

LX = 32
DEG = 4
COEF = (
    -5369.0 / 1800.0,
    12.0 / 7.0,
    -15.0 / 56.0,
    10.0 / 189.0,
    -1.0 / 112.0,
    2.0 / 1925.0,
    -1.0 / 16632.0,
)
INV_SPACING2 = 4.0
CENTRE = 24.0
HALF_WIDTH = 20.0
REACH = 6
MESH = pl.DeviceIdType.MESH
KINETIC = -0.5 * INV_SPACING2 / HALF_WIDTH
BLOCK = 128
GROUP = 8


def dot(a, b, dims=(((1,), (0,)), ((), ()))):
    return lax.dot_general(
        a, b, dims, precision=lax.Precision.HIGHEST, preferred_element_type=jnp.float32
    )


def exchange_kernel(axes, count, *refs):
    sources, targets = refs[:count], refs[count : 2 * count]
    send_sem, recv_sem, local_sem = refs[2 * count :]
    sizes = [lax.axis_size(a) for a in axes]
    total = int(np.prod(sizes))
    inner = total // sizes[0]
    me = lax.axis_index(axes[0])
    if len(axes) == 2:
        me = me * inner + lax.axis_index(axes[1])

    def peer_of(step):
        flat = lax.rem(me + step + 1, total)
        if len(axes) == 1:
            return flat, {axes[0]: flat}
        return flat, {axes[0]: lax.div(flat, inner), axes[1]: lax.rem(flat, inner)}

    barrier = pltpu.get_barrier_semaphore()

    def greet(step, carry):
        pl.semaphore_signal(barrier, inc=1, device_id=peer_of(step)[1], device_id_type=MESH)
        return carry

    lax.fori_loop(0, total - 1, greet, 0)
    pl.semaphore_wait(barrier, total - 1)

    def part(source, flat):
        return source.at[flat]

    def copies(step):
        flat, where = peer_of(step)
        return [
            pltpu.make_async_remote_copy(
                src_ref=part(s, flat),
                dst_ref=t.at[me],
                send_sem=send_sem.at[i, step],
                recv_sem=recv_sem.at[i, step],
                device_id=where,
                device_id_type=MESH,
            )
            for i, (s, t) in enumerate(zip(sources, targets))
        ]

    def begin(step, carry):
        for copy in copies(step):
            copy.start()
        return carry

    def finish(step, carry):
        for copy in copies(step):
            copy.wait()
        return carry

    lax.fori_loop(0, total - 1, begin, 0)
    own = [
        pltpu.make_async_copy(part(s, me), t.at[me], local_sem.at[i])
        for i, (s, t) in enumerate(zip(sources, targets))
    ]
    for copy in own:
        copy.start()
    for copy in own:
        copy.wait()
    lax.fori_loop(0, total - 1, finish, 0)


def exchange(arrays, axes, collective_id):
    total = int(np.prod([lax.axis_size(a) for a in axes]))
    count = len(arrays)
    return pl.pallas_call(
        functools.partial(exchange_kernel, axes, count),
        out_shape=[jax.ShapeDtypeStruct(a.shape, a.dtype) for a in arrays],
        in_specs=[pl.BlockSpec(memory_space=pl.ANY)] * count,
        out_specs=[pl.BlockSpec(memory_space=pl.ANY)] * count,
        scratch_shapes=[
            pltpu.SemaphoreType.DMA((count, total - 1)),
            pltpu.SemaphoreType.DMA((count, total - 1)),
            pltpu.SemaphoreType.DMA((count,)),
        ],
        compiler_params=pltpu.CompilerParams(
            collective_id=collective_id, has_side_effects=True
        ),
        name="exchange_" + "_".join(axes),
    )(*arrays)


def total_kernel(part_ref, out_ref, dom_in, dom_sum, band_in, own, sems):
    nd, nb = lax.axis_size("dom"), lax.axis_size("band")
    d, b = lax.axis_index("dom"), lax.axis_index("band")
    barrier = pltpu.get_barrier_semaphore()

    def greet(axis, me, size):
        def body(step, carry):
            pl.semaphore_signal(
                barrier, inc=1, device_id={axis: lax.rem(me + step + 1, size)}, device_id_type=MESH
            )
            return carry

        lax.fori_loop(0, size - 1, body, 0)

    greet("dom", d, nd)
    greet("band", b, nb)
    pl.semaphore_wait(barrier, nd + nb - 2)

    def phase(axis, me, size, base, source_of, target):
        def copy(step):
            peer = lax.rem(me + step + 1, size)
            return pltpu.make_async_remote_copy(
                src_ref=source_of(peer),
                dst_ref=target.at[me],
                send_sem=sems.at[0, base + step],
                recv_sem=sems.at[1, base + step],
                device_id={axis: peer},
                device_id_type=MESH,
            )

        def begin(step, carry):
            copy(step).start()
            return carry

        def finish(step, carry):
            copy(step).wait()
            return carry

        lax.fori_loop(0, size - 1, begin, 0)
        return lambda: lax.fori_loop(0, size - 1, finish, 0)

    done = phase("dom", d, nd, 0, lambda peer: part_ref.at[peer], dom_in)
    dom_in[d] = part_ref[d]
    done()
    dom_sum[...] = jnp.sum(dom_in[...], axis=0)
    done = phase("band", b, nb, nd, lambda peer: dom_sum.at[peer], band_in)
    band_in[b] = dom_sum[b]
    done()
    own[b] = jnp.sum(band_in[...], axis=0)
    phase("band", b, nb, nd + nb, lambda peer: own.at[b], own)()
    out_ref[d] = own[...]
    phase("dom", d, nd, nd + 2 * nb, lambda peer: out_ref.at[d], out_ref)()


def total_over_all(partial, collective_id):
    nd, nb = lax.axis_size("dom"), lax.axis_size("band")
    rows, columns = partial.shape
    piece = rows // (nd * nb)
    vmem = pl.BlockSpec(memory_space=pltpu.VMEM)
    out = pl.pallas_call(
        total_kernel,
        out_shape=jax.ShapeDtypeStruct((nd, nb, piece, columns), jnp.float32),
        in_specs=[vmem],
        out_specs=vmem,
        scratch_shapes=[
            pltpu.VMEM((nd, nb, piece, columns), jnp.float32),
            pltpu.VMEM((nb, piece, columns), jnp.float32),
            pltpu.VMEM((nb, piece, columns), jnp.float32),
            pltpu.VMEM((nb, piece, columns), jnp.float32),
            pltpu.SemaphoreType.DMA((2, 2 * (nd + nb))),
        ],
        compiler_params=pltpu.CompilerParams(
            collective_id=collective_id,
            has_side_effects=True,
            vmem_limit_bytes=48 * 1024 * 1024,
        ),
        name="gram_total",
    )(partial.reshape(nd, nb, piece, columns))
    return out.reshape(rows, columns)


def plane_matrix(cells):
    rows = cells // LX
    matrix = np.zeros((cells, cells), np.float64)
    index = np.arange(cells)
    y, x = index // LX, index % LX
    for step in range(1, REACH + 1):
        for sign in (step, -step):
            np.add.at(matrix, (y * LX + (x + sign) % LX, index), COEF[step])
            np.add.at(matrix, (((y + sign) % rows) * LX + x, index), COEF[step])
    return (KINETIC * matrix).astype(np.float32)


def filter_kernel(per_layer, splits, psi_ref, pot_ref, plane_ref, out_ref, one, two):
    rows, cells = psi_ref.shape
    edge = REACH * per_layer
    chunk = rows // max(1, rows // 192)
    width = cells // splits
    for buffer in (one, two):
        buffer[:edge] = jnp.zeros((edge, cells), jnp.float32)
        buffer[edge + rows :] = jnp.zeros((edge, cells), jnp.float32)

    def chunks(body):
        if per_layer % GROUP == 0:
            lax.fori_loop(0, rows // chunk, body, 0)
        else:
            for i in range(rows // chunk):
                body(i, 0)

    def fill(i, carry):
        at = i * chunk
        one[pl.ds(edge + at, chunk)] = psi_ref[pl.ds(at, chunk)]
        return carry

    chunks(fill)

    def degree(step, current, previous):
        def body(i, carry):
            at = i * chunk
            here = current[pl.ds(edge + at, chunk)]
            scale = 3.0 * COEF[0] * KINETIC - CENTRE / HALF_WIDTH
            total = dot(here, plane_ref[...])
            total = total + here * (pot_ref[pl.ds(at, chunk)] * (1.0 / HALF_WIDTH) + scale)
            for k in range(1, REACH + 1):
                above = current[pl.ds(at + edge + k * per_layer, chunk)]
                below = current[pl.ds(at + edge - k * per_layer, chunk)]
                total = total + (KINETIC * COEF[k]) * (above + below)
            if step > 0:
                total = 2.0 * total - previous[pl.ds(edge + at, chunk)]
            if step < DEG - 1:
                previous[pl.ds(edge + at, chunk)] = total
            else:
                for s in range(splits):
                    out_ref[s, pl.ds(at, chunk)] = total[:, s * width : (s + 1) * width]
            return carry

        chunks(body)

    buffers = (one, two)
    for step in range(DEG):
        degree(step, buffers[step % 2], buffers[(step + 1) % 2])


def filtered_blocks(psi, potential, per_layer, splits):
    rows, cells = psi.shape
    edge = REACH * per_layer
    vmem = pl.BlockSpec(memory_space=pltpu.VMEM)
    return pl.pallas_call(
        functools.partial(filter_kernel, per_layer, splits),
        out_shape=jax.ShapeDtypeStruct((splits, rows, cells // splits), jnp.float32),
        in_specs=[vmem] * 3,
        out_specs=vmem,
        scratch_shapes=[pltpu.VMEM((rows + 2 * edge, cells), jnp.float32)] * 2,
        compiler_params=pltpu.CompilerParams(vmem_limit_bytes=48 * 1024 * 1024),
        name="chebyshev_filter",
    )(psi, potential, plane_matrix(cells))


def block_inverse(block):
    count = BLOCK // GROUP
    column = lax.broadcasted_iota(jnp.int32, (GROUP, BLOCK), 1)
    row = lax.broadcasted_iota(jnp.int32, (GROUP, BLOCK), 0)
    left = [block[GROUP * g : GROUP * (g + 1)] for g in range(count)]
    right = [(column == row + GROUP * g).astype(jnp.float32) for g in range(count)]
    result = []
    for g in range(count):
        a, e = left[g], right[g]
        first = GROUP * g
        cols = [
            jnp.broadcast_to(a[:, first + k : first + k + 1], (GROUP, BLOCK))
            for k in range(GROUP)
        ]
        pivots = jnp.ones((GROUP, BLOCK), jnp.float32)
        for j in range(GROUP):
            pivot = jnp.broadcast_to(cols[j][j : j + 1], (GROUP, BLOCK))
            factor = jnp.where(row > j, cols[j] / pivot, 0.0)
            for k in range(j + 1, GROUP):
                cols[k] = cols[k] - factor * cols[k][j : j + 1]
            a = a - factor * a[j : j + 1]
            e = e - factor * e[j : j + 1]
            pivots = jnp.where(row == j, pivot, pivots)
        result.append(e * lax.rsqrt(pivots))
        if g + 1 < count:
            weights = (a / pivots).T
            for h in range(g + 1, count):
                piece = weights[GROUP * h : GROUP * (h + 1)]
                new_a, new_e = left[h], right[h]
                for k in range(GROUP):
                    w = piece[:, k : k + 1]
                    new_a = new_a - w * a[k : k + 1]
                    new_e = new_e - w * e[k : k + 1]
                left[h], right[h] = new_a, new_e
    return jnp.concatenate(result, axis=0)


def inverse_factor_kernel(scale, gram_ref, out_ref, work, rest):
    size = gram_ref.shape[0]
    work[...] = gram_ref[...] * scale
    row = lax.broadcasted_iota(jnp.int32, (size, size), 0)
    col = lax.broadcasted_iota(jnp.int32, (size, size), 1)
    rest[...] = (row == col).astype(jnp.float32)
    over_rows = (((0,), (0,)), ((), ()))

    def body(k, carry):
        at = pl.multiple_of(k * BLOCK, BLOCK)
        rows = pl.ds(at, BLOCK)
        inverse = block_inverse(work[rows, pl.ds(at, BLOCK)])
        upper = dot(inverse, work[rows, :])
        final = dot(inverse, rest[rows, :])
        out_ref[rows, :] = final
        work[...] -= dot(upper, upper, over_rows)
        rest[...] -= dot(upper, final, over_rows)
        return carry

    lax.fori_loop(0, size // BLOCK, body, 0)


def inverse_factor(gram, scale):
    vmem = pl.BlockSpec(memory_space=pltpu.VMEM)
    return pl.pallas_call(
        functools.partial(inverse_factor_kernel, scale),
        out_shape=jax.ShapeDtypeStruct(gram.shape, jnp.float32),
        in_specs=[vmem],
        out_specs=vmem,
        scratch_shapes=[pltpu.VMEM(gram.shape, jnp.float32)] * 2,
        compiler_params=pltpu.CompilerParams(vmem_limit_bytes=48 * 1024 * 1024),
        name="inverse_factor",
    )(gram)


def shards(psi, potential):
    nd, nb = lax.axis_size("dom"), lax.axis_size("band")
    bands, depth, cells = psi.shape
    mine = bands // nd
    width = cells // nb
    all_bands = bands * nb
    layers = depth * nd
    blocks = psi.reshape(nd, mine, depth, cells).transpose(0, 2, 1, 3)
    pots = jnp.broadcast_to(potential.reshape(1, depth, 1, cells), (nd, depth, 1, cells))
    blocks, pots = exchange([blocks, pots], ("dom",), 0)
    rows = blocks.reshape(layers * mine, cells)
    pot_rows = jnp.broadcast_to(
        pots.reshape(layers, 1, cells), (layers, mine, cells)
    ).reshape(layers * mine, cells)
    filtered = filtered_blocks(rows, pot_rows, mine, nb)
    pieces = filtered.reshape(nb * nd, depth, mine, width)
    (pieces,) = exchange([pieces], ("band", "dom"), 1)
    spread = pieces.transpose(0, 2, 1, 3).reshape(all_bands, depth * width)
    partial_gram = dot(spread, spread, (((1,), (1,)), ((), ())))
    gram = total_over_all(partial_gram, 2)
    inverse = inverse_factor(gram, 1.0 / (layers * cells))
    solved = dot(inverse, spread)
    (back,) = exchange([solved.reshape(nb, bands, depth * width)], ("band",), 3)
    back = back.reshape(nb, bands, depth, width).transpose(1, 2, 0, 3)
    return back.reshape(psi.shape)


def solution(mesh):
    placed = (P("band", "dom", None), P("dom", None))
    return jax.shard_map(
        shards, mesh=mesh, in_specs=placed, out_specs=P("band", "dom", None), check_vma=False
    )
```

time: 774 us -> 215 us (0.28); the launches traced: 764 us -> 214 us
  other arithmetic: 259 us -> 1.25 us
  local copies, waits for them, and re-layouts: 208 us -> 15 us
  Pallas kernels: 0 us -> 188 us
  waiting for transfers between devices: 163 us -> 0 us
  blocking collectives: 77.3 us -> 0 us
  starting transfers between devices: 22.7 us -> 0 us
  between operations: 16.6 us -> 0.13 us
  matrix products: 18.2 us -> 9.85 us
    pallas_call x0 -> x6, Pallas kernels: none -> 188 us  [the longest x3 95.5 us: exchange(): pl.pallas_call(functools.partial(exchange_kernel, axes, count), out_shape...]
    slice x144 -> x0, local copies, waits for them, and re-layouts: 181 us -> none  [the longest x48 60.8 us: shift_y(): return jnp.roll(values, step * LX, 2)]
    psum x1 -> x0, waiting for transfers between devices: 152 us -> none  [shards(): gram = lax.psum(partial_gram, ('dom', 'band')) / all_points]
    another operation x18 -> x0, other arithmetic: 119 us -> none  [the longest x14 78.8 us: shards(): lower = jnp.linalg.cholesky(gram)]
    sub x3 -> x0, other arithmetic: 102 us -> none  [chebyshev(): 2.0 * (hamiltonian(current, potential) - CENTRE * current) / HALF_WIDTH]
    all_to_all x2 -> x0, blocking collectives: 77.3 us -> none  [the longest x1 38.6 us: shards(): lax.all_to_all(flatrows, 'band', split_axis=1, concat_axis=0, tiled=True)]
    div x3 -> x0, other arithmetic: 34.8 us -> none  [the longest x1 31 us: chebyshev(): current = (hamiltonian(start, potential) - CENTRE * start) / HALF_WIDTH]
    ppermute x8 -> x0, starting transfers between devices: 22.7 us -> none  [the longest x4 14.4 us: with_halo(): lax.ppermute(lax.slice_in_dim(block, block.shape[dim] - width, None, axis...]
  transfers between devices with their start and end apart: 9 -> 0, of which waited for: 3 -> 0; matrix products, arithmetic and copies ran while one was open for 14% -> 0% of each run, Pallas kernels for 0% -> 0%
where the time goes in v1:
time: 215 us; the launch traced here: 214 us
  Pallas kernels  188 us (87%)
  local copies, waits for them, and re-layouts  15 us (7%)
  matrix products  9.85 us (5%)
    pallas_call x3, Pallas kernels, exchange(): pl.pallas_call(functools.partial(exchange_kernel, axes, count), out_shape...  95.5 us
    pallas_call x1, Pallas kernels, total_over_all(): pl.pallas_call(total_kernel, out_shape=jax.ShapeDtypeStruct((nd, nb, piec...  42 us
    pallas_call x1, Pallas kernels, inverse_factor(): pl.pallas_call(functools.partial(inverse_factor_kernel, scale), out_shape...  32.2 us
    pallas_call x1, Pallas kernels, filtered_blocks(): pl.pallas_call(functools.partial(filter_kernel, per_layer, splits), out_s...  18.1 us
    dot_general x2, matrix products, dot(): lax.dot_general(a, b, dims, precision=lax.Precision.HIGHEST, preferred_el...  9.85 us

profile of v1, /device:TPU:25, one launch (start us, length us, event | category | flops | bytes accessed | tf_op | source)
XLA Modules:
  0.0 213.9 jit_solution(14650372605791696872)
XLA Ops:
  0.0 2.8 %copy.18 = f32[8,16,6,512]{3,1,2,0:T(8,128)} copy(f32[8,16,6,512]{3,1,0,2:T(8,128)} %bitcast.29) | data formatting | bytes 3145728 | tf_op jit(solution)/shard_map/reshape | solution.py:359
  2.8 0.0 copy-done.3
  2.8 0.7 broadcast_in_dim.12.refs_1_
  3.5 22.5 %exchange_dom.1 = (f32[8,6,16,512]{3,2,1,0:T(8,128)}, f32[8,6,1,512]{3,2,1,0:T(1,128)}) custom-call(f32[8,6,16,512]{3,2,1,0:T(8,128)} %bitcast.25, f32[8,6,1,512]{3,2,1,0:T(1,128)} %broadcast_in_dim.12.refs_1_), custom_call_target="tpu_custom_call" | custom-call | tf_op jit(solution)/shard_map/exchange_dom/pallas_call | solution.py:105
  26.0 0.0 copy-start.1
  26.0 1.2 reduce
  27.3 0.2 broadcast_in_dim.14
  27.5 0.0 copy-done.2
  27.5 18.1 %chebyshev_filter.1 = f32[4,768,128]{2,1,0:T(8,128)S(1)} custom-call(f32[768,512]{1,0:T(8,128)S(1)} %bitcast.24, f32[768,512]{1,0:T(8,128)S(1)} %bitcast.20, f32[512,512]{1,0:T(8,128)S(1)} %copy-done.2), custom_call_target="tpu_custom_call" | custom-call | tf_op jit(solution)/shard_map/chebyshev_filter/pallas_call | solution.py:269
  45.6 0.0 copy-start
  45.6 1.1 copy-done
  46.7 35.6 %exchange_band_dom.1 = f32[32,6,16,128]{3,2,1,0:T(8,128)} custom-call(f32[32,6,16,128]{3,2,1,0:T(8,128)} %bitcast.21), custom_call_target="tpu_custom_call" | custom-call | tf_op jit(solution)/shard_map/exchange_band_dom/pallas_call | solution.py:105
  82.3 2.0 copy.10
  84.3 1.5 dot_general.10
  85.8 1.5 reshape.43
  87.4 4.6 %fusion.part_ref = f32[8,4,16,512]{3,2,1,0:T(8,128)S(1)} fusion(f32[8,4,16,768]{3,2,1,0:T(8,128)} %dot_general.10, f32[512,768,1,1]{1,0,2,3:T(8,128)} %reshape.43), kind=kOutput, calls=%fused_computation | convolution fusion | flops 2415919104 | bytes 4194304 | tf_op jit(solution)/shard_map/dot_general | solution.py:33
  91.9 42.0 %gram_total.1 = f32[8,4,16,512]{3,2,1,0:T(8,128)S(1)} custom-call(f32[8,4,16,512]{3,2,1,0:T(8,128)S(1)} %fusion.part_ref), custom_call_target="tpu_custom_call" | custom-call | tf_op jit(solution)/shard_map/gram_total/pallas_call | solution.py:181
  133.9 32.2 %inverse_factor.1 = f32[512,512]{1,0:T(8,128)S(1)} custom-call(f32[512,512]{1,0:T(8,128)S(1)} %bitcast.22), custom_call_target="tpu_custom_call" | custom-call | tf_op jit(solution)/shard_map/inverse_factor/pallas_call | solution.py:341
  166.1 1.5 reshape.44
  167.6 5.3 %fusion.2.refs_0_ = f32[4,128,768]{2,1,0:T(8,128)} fusion(f32[4,128,512]{2,1,0:T(8,128)S(1)} %bitcast.23, f32[512,768,1]{1,0,2:T(8,128)} %reshape.44), kind=kOutput, calls=%fused_computation.3 | convolution fusion | flops 2415919104 | bytes 4194304 | tf_op jit(solution)/shard_map/dot_general | solution.py:33
  172.9 37.4 %exchange_band.1 = f32[4,128,768]{2,1,0:T(8,128)} custom-call(f32[4,128,768]{2,1,0:T(8,128)} %fusion.2.refs_0_), custom_call_target="tpu_custom_call" | custom-call | tf_op jit(solution)/shard_map/exchange_band/pallas_call | solution.py:105
  210.3 1.9 copy.12
  212.2 0.2 copy.13
  212.3 1.6 copy.14
  (4 shorter events, 0.0 us)
Async XLA Ops:
  0.0 2.8 %copy-start.3 = (f32[6,512]{1,0:T(8,128)S(1)}, f32[6,512]{1,0:T(8,128)}, u32[]{:S(2)}) copy-start(f32[6,512]{1,0:T(8,128)} %param.4) | copy-start | bytes 36868
  3.5 24.0 %copy-start.2 = (f32[512,512]{1,0:T(8,128)S(1)}, f32[512,512]{1,0:T(8,128)}, u32[]{:S(2)}) copy-start(f32[512,512]{1,0:T(8,128)} %constant.2.clone.plane_ref) | copy-start | bytes 3145732
  26.0 1.5 copy-start.1
  45.6 1.1 copy-start

commit v2 on v1

--- a/solution.py
+++ b/solution.py
@@ -349,7 +349,356 @@
     )(gram)
 
 
+def upper_layout(size):
+    count = size // BLOCK
+    half = count // 2
+    places = []
+    for i in range(count):
+        length = size - i * BLOCK
+        if i < half:
+            places.append((i, 0, length))
+        else:
+            places.append((count - 1 - i, size - (count - 1 - i) * BLOCK, length))
+    return places
+
+
+def neighbours(axis):
+    size, me = lax.axis_size(axis), lax.axis_index(axis)
+    return size, me, lambda step: lax.rem(me + step + 1, size)
+
+
+def repeat(count, body):
+    def step_of(step, carry):
+        body(step)
+        return carry
+
+    lax.fori_loop(0, count, step_of, 0)
+
+
+def gram_kernel(
+    mine, psi_ref, pot_ref, plane_ref, spread_ref, gram_ref,
+    one, two, diagonal, pots, sent, landed, dom_in, dom_sum, band_in, own, partial,
+    dom_sems, pot_sems, all_sems, sum_sems, local_sems,
+):
+    depth, _, cells = psi_ref.shape
+    nd, d, dom_peer = neighbours("dom")
+    nb, b, band_peer = neighbours("band")
+    total = nd * nb
+    me = b * nd + d
+    halves = mine // GROUP
+    layers = depth * nd
+    width = cells // nb
+    bands = mine * total
+
+    def device(step):
+        flat = lax.rem(me + step + 1, total)
+        return lax.div(flat, nd), lax.rem(flat, nd)
+
+    def place(step):
+        to_b, to_d = device(step)
+        return {"band": to_b, "dom": to_d}
+
+    barrier = pltpu.get_barrier_semaphore()
+
+    @functools.partial(repeat, total - 1)
+    def _(step):
+        pl.semaphore_signal(barrier, inc=1, device_id=place(step), device_id_type=MESH)
+
+    for h in range(halves):
+        for buffer in (one, two):
+            buffer[h, :REACH] = jnp.zeros((REACH, GROUP, cells), jnp.float32)
+            buffer[h, REACH + layers :] = jnp.zeros((REACH, GROUP, cells), jnp.float32)
+    pl.semaphore_wait(barrier, total - 1)
+
+    def potential_copy(step):
+        return pltpu.make_async_remote_copy(
+            src_ref=pot_ref,
+            dst_ref=pots.at[d],
+            send_sem=pot_sems.at[0, step],
+            recv_sem=pot_sems.at[1, step],
+            device_id={"dom": dom_peer(step)},
+            device_id_type=MESH,
+        )
+
+    def band_rows(owner, h):
+        start = pl.multiple_of(owner * mine + h * GROUP, GROUP)
+        return psi_ref.at[:, pl.ds(start, GROUP), :]
+
+    def own_layers(h):
+        return one.at[h, pl.ds(REACH + depth * d, depth)]
+
+    def column_copy(h, step):
+        return pltpu.make_async_remote_copy(
+            src_ref=band_rows(dom_peer(step), h),
+            dst_ref=own_layers(h),
+            send_sem=dom_sems.at[0, h, step],
+            recv_sem=dom_sems.at[1, h, step],
+            device_id={"dom": dom_peer(step)},
+            device_id_type=MESH,
+        )
+
+    repeat(nd - 1, lambda step: potential_copy(step).start())
+    local = [pltpu.make_async_copy(pot_ref, pots.at[d], local_sems.at[0])]
+    for h in range(halves):
+        repeat(nd - 1, lambda step, h=h: column_copy(h, step).start())
+        local.append(pltpu.make_async_copy(band_rows(d, h), own_layers(h), local_sems.at[1 + h]))
+    for copy in local:
+        copy.start()
+    for copy in local:
+        copy.wait()
+    repeat(nd - 1, lambda step: potential_copy(step).wait())
+    scale = 3.0 * COEF[0] * KINETIC - CENTRE / HALF_WIDTH
+    for owner in range(nd):
+        rows = pots[owner] * (1.0 / HALF_WIDTH) + scale
+        for layer in range(depth):
+            diagonal[owner * depth + layer] = jnp.broadcast_to(
+                rows[layer : layer + 1], (GROUP, cells)
+            )
+
+    chunk = layers // 2
+
+    def degree(h, step, current, previous):
+        def body(i):
+            at = i * chunk
+            here = current[h, pl.ds(REACH + at, chunk)]
+            flat = here.reshape(chunk * GROUP, cells)
+            total = dot(flat, plane_ref[...]).reshape(here.shape)
+            total = total + here * diagonal[pl.ds(at, chunk)]
+            for k in range(1, REACH + 1):
+                above = current[h, pl.ds(REACH + at + k, chunk)]
+                below = current[h, pl.ds(REACH + at - k, chunk)]
+                total = total + (KINETIC * COEF[k]) * (above + below)
+            if step > 0:
+                total = 2.0 * total - previous[h, pl.ds(REACH + at, chunk)]
+            if step < DEG - 1:
+                previous[h, pl.ds(REACH + at, chunk)] = total
+            else:
+                for s in range(nb):
+                    sent[h, s, pl.ds(at, chunk)] = total[:, :, s * width : (s + 1) * width]
+
+        repeat(layers // chunk, body)
+
+    def point_copy(h, step):
+        to_b, to_d = device(step)
+        return pltpu.make_async_remote_copy(
+            src_ref=sent.at[h, to_b, pl.ds(to_d * depth, depth)],
+            dst_ref=landed.at[me * halves + h],
+            send_sem=all_sems.at[0, h, step],
+            recv_sem=all_sems.at[1, h, step],
+            device_id={"band": to_b, "dom": to_d},
+            device_id_type=MESH,
+        )
+
+    buffers = (one, two)
+    for h in range(halves):
+        repeat(nd - 1, lambda step, h=h: column_copy(h, step).wait())
+        for step in range(DEG):
+            degree(h, step, buffers[step % 2], buffers[(step + 1) % 2])
+        repeat(total - 1, lambda step, h=h: point_copy(h, step).start())
+        landed[me * halves + h] = sent[h, b, pl.ds(d * depth, depth)]
+    for h in range(halves):
+        repeat(total - 1, lambda step, h=h: point_copy(h, step).wait())
+    for layer in range(depth):
+        spread_ref[:, layer * width : (layer + 1) * width] = landed[:, layer].reshape(bands, width)
+
+    tiles = BLOCK // GROUP
+    for i, (row, column, length) in enumerate(upper_layout(bands)):
+        block = dot(
+            spread_ref[i * BLOCK : (i + 1) * BLOCK, :],
+            spread_ref[i * BLOCK :, :],
+            (((1,), (1,)), ((), ())),
+        )
+        partial[row * tiles : (row + 1) * tiles, :, column : column + length] = block.reshape(
+            tiles, GROUP, length
+        )
+
+    def pieces(ref, owner):
+        return ref.at[pl.ds(owner * nb, nb)]
+
+    def phase(axis, me, size, peer_of, base, source_of, target):
+        def copy(step):
+            return pltpu.make_async_remote_copy(
+                src_ref=source_of(peer_of(step)),
+                dst_ref=target,
+                send_sem=sum_sems.at[0, base + step],
+                recv_sem=sum_sems.at[1, base + step],
+                device_id={axis: peer_of(step)},
+                device_id_type=MESH,
+            )
+
+        repeat(size - 1, lambda step: copy(step).start())
+        return lambda: repeat(size - 1, lambda step: copy(step).wait())
+
+    done = phase("dom", d, nd, dom_peer, 0, lambda peer: pieces(partial, peer), dom_in.at[d])
+    dom_in[d] = partial[pl.ds(d * nb, nb)]
+    done()
+    dom_sum[...] = jnp.sum(dom_in[...], axis=0)
+    done = phase("band", b, nb, band_peer, nd, lambda peer: dom_sum.at[peer], band_in.at[b])
+    band_in[b] = dom_sum[b]
+    done()
+    own[b] = jnp.sum(band_in[...], axis=0)
+    phase("band", b, nb, band_peer, nd + nb, lambda peer: own.at[b], own.at[b])()
+    gram_ref[pl.ds(d * nb, nb)] = own[...]
+    phase(
+        "dom", d, nd, dom_peer, nd + 2 * nb, lambda peer: pieces(gram_ref, d), pieces(gram_ref, d)
+    )()
+
+
+def spread_and_gram(psi, potential):
+    depth, held, cells = psi.shape
+    nd, nb = lax.axis_size("dom"), lax.axis_size("band")
+    total, mine, layers, width = nd * nb, held // nd, depth * nd, cells // nb
+    halves, bands = mine // GROUP, held * nb
+    columns = bands + BLOCK
+    f32 = jnp.float32
+    vmem, where = pl.BlockSpec(memory_space=pltpu.VMEM), pl.BlockSpec(memory_space=pl.ANY)
+    padded = pltpu.VMEM((halves, layers + 2 * REACH, GROUP, cells), f32)
+    piece = (GROUP, columns)
+    dma = pltpu.SemaphoreType.DMA
+    return pl.pallas_call(
+        functools.partial(gram_kernel, mine),
+        out_shape=[
+            jax.ShapeDtypeStruct((bands, depth * width), f32),
+            jax.ShapeDtypeStruct((total, *piece), f32),
+        ],
+        in_specs=[where, vmem, vmem],
+        out_specs=[vmem, vmem],
+        scratch_shapes=[
+            padded,
+            padded,
+            pltpu.VMEM((layers, GROUP, cells), f32),
+            pltpu.VMEM((nd, depth, cells), f32),
+            pltpu.VMEM((halves, nb, layers, GROUP, width), f32),
+            pltpu.VMEM((total * halves, depth, GROUP, width), f32),
+            pltpu.VMEM((nd, nb, *piece), f32),
+            pltpu.VMEM((nb, *piece), f32),
+            pltpu.VMEM((nb, *piece), f32),
+            pltpu.VMEM((nb, *piece), f32),
+            pltpu.VMEM((total, *piece), f32),
+            dma((2, halves, nd - 1)),
+            dma((2, nd - 1)),
+            dma((2, halves, total - 1)),
+            dma((2, 2 * (nd + nb))),
+            dma((1 + halves,)),
+        ],
+        compiler_params=pltpu.CompilerParams(
+            collective_id=0, has_side_effects=True, vmem_limit_bytes=56 * 1024 * 1024
+        ),
+        name="filter_gram",
+    )(psi, potential, plane_matrix(cells))
+
+
+def solve_kernel(scale, gram_ref, spread_ref, out_ref, work, rest, ready, sems, local_sem):
+    size = spread_ref.shape[0]
+    depth, held, cells = out_ref.shape
+    nb, b, band_peer = neighbours("band")
+    width = cells // nb
+    barrier = pltpu.get_barrier_semaphore()
+
+    @functools.partial(repeat, nb - 1)
+    def _(step):
+        pl.semaphore_signal(
+            barrier, inc=1, device_id={"band": band_peer(step)}, device_id_type=MESH
+        )
+
+    work[...] = jnp.zeros_like(work)
+    tiles = BLOCK // GROUP
+    for i, (row, column, length) in enumerate(upper_layout(size)):
+        packed = gram_ref[row * tiles : (row + 1) * tiles, :, column : column + length]
+        work[i * BLOCK : (i + 1) * BLOCK, i * BLOCK :] = packed.reshape(BLOCK, length) * scale
+    row = lax.broadcasted_iota(jnp.int32, (size, size), 0)
+    col = lax.broadcasted_iota(jnp.int32, (size, size), 1)
+    rest[...] = (row == col).astype(jnp.float32)
+    over_rows = (((0,), (0,)), ((), ()))
+    pl.semaphore_wait(barrier, nb - 1)
+
+    def points(ref, owner):
+        return ref.at[:, :, pl.ds(pl.multiple_of(owner * width, 128), width)]
+
+    def copy(target, source):
+        return pltpu.make_async_remote_copy(
+            src_ref=ready.at[target],
+            dst_ref=points(out_ref, b),
+            send_sem=sems.at[0, target],
+            recv_sem=sems.at[1, source],
+            device_id={"band": target},
+            device_id_type=MESH,
+        )
+
+    def body(k):
+        at = pl.multiple_of(k * BLOCK, BLOCK)
+        rows = pl.ds(at, BLOCK)
+        inverse = block_inverse(work[rows, pl.ds(at, BLOCK)])
+        final = dot(inverse, rest[rows, :])
+        solved = dot(final, spread_ref[...])
+        for part in range(BLOCK // held):
+            target = k * (BLOCK // held) + part
+            for layer in range(depth):
+                ready[target, layer] = solved[
+                    part * held : (part + 1) * held, layer * width : (layer + 1) * width
+                ]
+
+            @pl.when(target != b)
+            def _():
+                copy(target, b).start()
+
+        upper = dot(inverse, work[rows, :])
+        work[...] -= dot(upper, upper, over_rows)
+        rest[...] -= dot(upper, final, over_rows)
+
+    repeat(size // BLOCK, body)
+    own = pltpu.make_async_copy(ready.at[b], points(out_ref, b), local_sem)
+    own.start()
+    own.wait()
+
+    @functools.partial(repeat, nb - 1)
+    def _(step):
+        copy(band_peer(step), band_peer(step)).wait()
+
+
+def solved_basis(gram, spread, shape, scale):
+    depth, held, cells = shape
+    nb = lax.axis_size("band")
+    size = spread.shape[0]
+    vmem = pl.BlockSpec(memory_space=pltpu.VMEM)
+    return pl.pallas_call(
+        functools.partial(solve_kernel, scale),
+        out_shape=jax.ShapeDtypeStruct(shape, jnp.float32),
+        in_specs=[vmem, vmem],
+        out_specs=pl.BlockSpec(memory_space=pl.ANY),
+        scratch_shapes=[
+            pltpu.VMEM((size, size), jnp.float32),
+            pltpu.VMEM((size, size), jnp.float32),
+            pltpu.VMEM((nb, depth, held, cells // nb), jnp.float32),
+            pltpu.SemaphoreType.DMA((2, nb)),
+            pltpu.SemaphoreType.DMA,
+        ],
+        compiler_params=pltpu.CompilerParams(
+            collective_id=1, has_side_effects=True, vmem_limit_bytes=48 * 1024 * 1024
+        ),
+        name="factor_solve",
+    )(gram, spread)
+
+
 def shards(psi, potential):
+    bands, depth, cells = psi.shape
+    nd, nb = lax.axis_size("dom"), lax.axis_size("band")
+    aligned = (
+        bands % (nd * GROUP) == 0
+        and cells % (nb * 128) == 0
+        and BLOCK % bands == 0
+        and bands * nb == GROUP * nd * nb * 2
+        and bands * nb == 4 * BLOCK
+    )
+    if not aligned:
+        return staged(psi, potential)
+    spread, gram = spread_and_gram(psi.transpose(1, 0, 2), potential)
+    scale = 1.0 / (depth * nd * cells)
+    out = solved_basis(gram, spread, (depth, bands, cells), scale)
+    return out.transpose(1, 0, 2)
+
+
+def staged(psi, potential):
     nd, nb = lax.axis_size("dom"), lax.axis_size("band")
     bands, depth, cells = psi.shape
     mine = bands // nd

time: 215 us -> 160 us (0.74)
  Pallas kernels: 188 us -> 156 us
  local copies, waits for them, and re-layouts: 15 us -> 3.63 us
  matrix products: 9.85 us -> 0 us
    pallas_call x6 -> x2, Pallas kernels: 188 us -> 156 us  [the longest x1 93.4 us: spread_and_gram(): pl.pallas_call(functools.partial(gram_kernel, mine), out_shape=[jax.Shape...]
    dot_general x2 -> x0, matrix products: 9.85 us -> none  [dot(): lax.dot_general(a, b, dims, precision=lax.Precision.HIGHEST, preferred_el...]
    reshape x4 -> x0, local copies, waits for them, and re-layouts: 7.43 us -> none  [the longest x2 3.03 us: shards(): spread = pieces.transpose(0, 2, 1, 3).reshape(all_bands, depth * width)]
    unnamed x8 -> x5, local copies, waits for them, and re-layouts: 1.15 us -> 3.63 us
    transpose x2 -> x0, local copies, waits for them, and re-layouts: 2.18 us -> none  [the longest x1 2.03 us: shards(): spread = pieces.transpose(0, 2, 1, 3).reshape(all_bands, depth * width)]
where the time goes in v2:
time: 160 us
  Pallas kernels  156 us (98%)
  local copies, waits for them, and re-layouts  3.63 us (2%)
    pallas_call x1, Pallas kernels, spread_and_gram(): pl.pallas_call(functools.partial(gram_kernel, mine), out_shape=[jax.Shape...  93.4 us
    pallas_call x1, Pallas kernels, solved_basis(): pl.pallas_call(functools.partial(solve_kernel, scale), out_shape=jax.Shap...  62.9 us
    unnamed x5, local copies, waits for them, and re-layouts  3.63 us

profile of v2, /device:TPU:25, one launch (start us, length us, event | category | flops | bytes accessed | tf_op | source)
XLA Modules:
  0.0 160.0 jit_solution(10121623745622636085)
XLA Ops:
  0.0 93.4 %filter_gram.1 = (f32[512,768]{1,0:T(8,128)}, f32[32,8,640]{2,1,0:T(8,128)}) custom-call(f32[6,128,512]{2,1,0:T(8,128)} %bitcast.3, f32[6,512]{1,0:T(8,128)} %pot_ref.1, f32[512,512]{1,0:T(8,128)} %constant.2.clone.plane_ref), custom_call_target="tpu_custom_call" | custom-call | tf_op jit(solution)/shard_map/filter_gram/pallas_call | solution.py:558
  93.4 0.0 copy-start
  93.4 1.4 copy-done
  94.8 0.0 copy-start.1
  94.8 1.1 copy-done.1
  95.9 62.9 %factor_solve.1 = f32[6,128,512]{2,1,0:T(8,128)S(1)} custom-call(f32[32,8,640]{2,1,0:T(8,128)S(1)} %copy-done.1, f32[512,768]{1,0:T(8,128)S(1)} %copy-done), custom_call_target="tpu_custom_call" | custom-call | tf_op jit(solution)/shard_map/factor_solve/pallas_call | solution.py:664
  158.8 1.1 copy.5
Async XLA Ops:
  93.4 1.4 copy-start
  94.8 1.1 copy-start.1

commit v3 on v2

--- a/solution.py
+++ b/solution.py
@@ -375,10 +375,11 @@
     lax.fori_loop(0, count, step_of, 0)
 
 
-def gram_kernel(
-    mine, psi_ref, pot_ref, plane_ref, spread_ref, gram_ref,
+def whole_kernel(
+    mine, psi_ref, pot_ref, plane_ref, out_ref,
     one, two, diagonal, pots, sent, landed, dom_in, dom_sum, band_in, own, partial,
-    dom_sems, pot_sems, all_sems, sum_sems, local_sems,
+    spread_ref, gram_ref, work, rest, inverses, ready, arrived, placed,
+    dom_sems, pot_sems, all_sems, sum_sems, solve_sems, local_sems,
 ):
     depth, _, cells = psi_ref.shape
     nd, d, dom_peer = neighbours("dom")
@@ -501,21 +502,20 @@
     for layer in range(depth):
         spread_ref[:, layer * width : (layer + 1) * width] = landed[:, layer].reshape(bands, width)
 
-    tiles = BLOCK // GROUP
-    for i, (row, column, length) in enumerate(upper_layout(bands)):
-        block = dot(
-            spread_ref[i * BLOCK : (i + 1) * BLOCK, :],
-            spread_ref[i * BLOCK :, :],
-            (((1,), (1,)), ((), ())),
-        )
-        partial[row * tiles : (row + 1) * tiles, :, column : column + length] = block.reshape(
-            tiles, GROUP, length
-        )
-
     def pieces(ref, owner):
         return ref.at[pl.ds(owner * nb, nb)]
 
-    def phase(axis, me, size, peer_of, base, source_of, target):
+    def gram_copy(target, source):
+        return pltpu.make_async_remote_copy(
+            src_ref=pieces(partial, target),
+            dst_ref=dom_in.at[d],
+            send_sem=sum_sems.at[0, target],
+            recv_sem=sum_sems.at[1, source],
+            device_id={"dom": target},
+            device_id_type=MESH,
+        )
+
+    def phase(axis, size, peer_of, base, source_of, target):
         def copy(step):
             return pltpu.make_async_remote_copy(
                 src_ref=source_of(peer_of(step)),
@@ -529,26 +529,108 @@
         repeat(size - 1, lambda step: copy(step).start())
         return lambda: repeat(size - 1, lambda step: copy(step).wait())
 
-    done = phase("dom", d, nd, dom_peer, 0, lambda peer: pieces(partial, peer), dom_in.at[d])
+    tiles = BLOCK // GROUP
+    layout = upper_layout(bands)
+    for part in range(2):
+        for i, (row, column, length) in enumerate(layout):
+            if row == part:
+                block = dot(
+                    spread_ref[i * BLOCK : (i + 1) * BLOCK, :],
+                    spread_ref[i * BLOCK :, :],
+                    (((1,), (1,)), ((), ())),
+                )
+                partial[row * tiles : (row + 1) * tiles, :, column : column + length] = (
+                    block.reshape(tiles, GROUP, length)
+                )
+
+        @functools.partial(repeat, nd // 2)
+        def _(step, part=part):
+            target = part * (nd // 2) + step
+
+            @pl.when(target != d)
+            def _():
+                gram_copy(target, d).start()
+
     dom_in[d] = partial[pl.ds(d * nb, nb)]
-    done()
+    repeat(nd - 1, lambda step: gram_copy(dom_peer(step), dom_peer(step)).wait())
     dom_sum[...] = jnp.sum(dom_in[...], axis=0)
-    done = phase("band", b, nb, band_peer, nd, lambda peer: dom_sum.at[peer], band_in.at[b])
+    done = phase("band", nb, band_peer, nd, lambda peer: dom_sum.at[peer], band_in.at[b])
     band_in[b] = dom_sum[b]
     done()
     own[b] = jnp.sum(band_in[...], axis=0)
-    phase("band", b, nb, band_peer, nd + nb, lambda peer: own.at[b], own.at[b])()
+    phase("band", nb, band_peer, nd + nb, lambda peer: own.at[b], own.at[b])()
     gram_ref[pl.ds(d * nb, nb)] = own[...]
-    phase(
-        "dom", d, nd, dom_peer, nd + 2 * nb, lambda peer: pieces(gram_ref, d), pieces(gram_ref, d)
-    )()
-
-
-def spread_and_gram(psi, potential):
+    done = phase(
+        "dom", nd, dom_peer, nd + 2 * nb, lambda peer: pieces(gram_ref, d), pieces(gram_ref, d)
+    )
+    row_of = lax.broadcasted_iota(jnp.int32, (bands, bands), 0)
+    column_of = lax.broadcasted_iota(jnp.int32, (bands, bands), 1)
+    rest[...] = (row_of == column_of).astype(jnp.float32)
+    done()
+
+    def solve_copy(target, source):
+        return pltpu.make_async_remote_copy(
+            src_ref=ready.at[target],
+            dst_ref=arrived.at[b],
+            send_sem=solve_sems.at[0, target],
+            recv_sem=solve_sems.at[1, source],
+            device_id={"band": target},
+            device_id_type=MESH,
+        )
+
+    scale = 1.0 / (layers * cells)
+    for i, (row, column, length) in enumerate(layout):
+        packed = gram_ref[row * tiles : (row + 1) * tiles, :, column : column + length]
+        work[i * BLOCK : (i + 1) * BLOCK, i * BLOCK :] = packed.reshape(BLOCK, length) * scale
+    over_rows = (((0,), (0,)), ((), ()))
+    for k in range(nb):
+        low, high = k * BLOCK, (k + 1) * BLOCK
+        if k == 0:
+            ready[k] = spread_ref[:high]
+        else:
+            ready[k] = dot(rest[low:high, :high], spread_ref[:high])
+
+        @pl.when(b != k)
+        def _(k=k):
+            solve_copy(k, b).start()
+
+        inverse = block_inverse(work[low:high, low:high])
+        inverses[k] = inverse
+        if high < bands:
+            upper = dot(inverse, work[low:high, high:])
+            final = dot(inverse, rest[low:high, :high])
+            work[high:, high:] -= dot(upper, upper, over_rows)
+            rest[high:, :high] -= dot(upper, final, over_rows)
+
+    def points(ref, owner):
+        return ref.at[:, :, pl.ds(pl.multiple_of(owner * width, 128), width)]
+
+    def result_copy(owner):
+        return pltpu.make_async_copy(placed.at[owner], points(out_ref, owner), local_sems.at[owner])
+
+    def finish(owner, values):
+        solved = dot(inverses[b], values)
+        for layer in range(depth):
+            placed[owner, layer] = solved[:, layer * width : (layer + 1) * width]
+        result_copy(owner).start()
+
+    finish(b, ready[b])
+
+    @functools.partial(repeat, nb - 1)
+    def _(step):
+        peer = band_peer(step)
+        solve_copy(peer, peer).wait()
+        finish(peer, arrived[peer])
+
+    repeat(nb, lambda owner: result_copy(owner).wait())
+
+
+def whole(psi, potential):
     depth, held, cells = psi.shape
     nd, nb = lax.axis_size("dom"), lax.axis_size("band")
     total, mine, layers, width = nd * nb, held // nd, depth * nd, cells // nb
     halves, bands = mine // GROUP, held * nb
+    points = depth * width
     columns = bands + BLOCK
     f32 = jnp.float32
     vmem, where = pl.BlockSpec(memory_space=pltpu.VMEM), pl.BlockSpec(memory_space=pl.ANY)
@@ -556,13 +638,10 @@
     piece = (GROUP, columns)
     dma = pltpu.SemaphoreType.DMA
     return pl.pallas_call(
-        functools.partial(gram_kernel, mine),
-        out_shape=[
-            jax.ShapeDtypeStruct((bands, depth * width), f32),
-            jax.ShapeDtypeStruct((total, *piece), f32),
-        ],
+        functools.partial(whole_kernel, mine),
+        out_shape=jax.ShapeDtypeStruct(psi.shape, f32),
         in_specs=[where, vmem, vmem],
-        out_specs=[vmem, vmem],
+        out_specs=where,
         scratch_shapes=[
             padded,
             padded,
@@ -575,109 +654,26 @@
             pltpu.VMEM((nb, *piece), f32),
             pltpu.VMEM((nb, *piece), f32),
             pltpu.VMEM((total, *piece), f32),
+            pltpu.VMEM((bands, points), f32),
+            pltpu.VMEM((total, *piece), f32),
+            pltpu.VMEM((bands, bands), f32),
+            pltpu.VMEM((bands, bands), f32),
+            pltpu.VMEM((nb, BLOCK, BLOCK), f32),
+            pltpu.VMEM((nb, BLOCK, points), f32),
+            pltpu.VMEM((nb, BLOCK, points), f32),
+            pltpu.VMEM((nb, depth, BLOCK, width), f32),
             dma((2, halves, nd - 1)),
             dma((2, nd - 1)),
             dma((2, halves, total - 1)),
             dma((2, 2 * (nd + nb))),
-            dma((1 + halves,)),
+            dma((2, nb)),
+            dma((max(1 + halves, nb),)),
         ],
         compiler_params=pltpu.CompilerParams(
             collective_id=0, has_side_effects=True, vmem_limit_bytes=56 * 1024 * 1024
         ),
-        name="filter_gram",
+        name="filter_factor_solve",
     )(psi, potential, plane_matrix(cells))
-
-
-def solve_kernel(scale, gram_ref, spread_ref, out_ref, work, rest, ready, sems, local_sem):
-    size = spread_ref.shape[0]
-    depth, held, cells = out_ref.shape
-    nb, b, band_peer = neighbours("band")
-    width = cells // nb
-    barrier = pltpu.get_barrier_semaphore()
-
-    @functools.partial(repeat, nb - 1)
-    def _(step):
-        pl.semaphore_signal(
-            barrier, inc=1, device_id={"band": band_peer(step)}, device_id_type=MESH
-        )
-
-    work[...] = jnp.zeros_like(work)
-    tiles = BLOCK // GROUP
-    for i, (row, column, length) in enumerate(upper_layout(size)):
-        packed = gram_ref[row * tiles : (row + 1) * tiles, :, column : column + length]
-        work[i * BLOCK : (i + 1) * BLOCK, i * BLOCK :] = packed.reshape(BLOCK, length) * scale
-    row = lax.broadcasted_iota(jnp.int32, (size, size), 0)
-    col = lax.broadcasted_iota(jnp.int32, (size, size), 1)
-    rest[...] = (row == col).astype(jnp.float32)
-    over_rows = (((0,), (0,)), ((), ()))
-    pl.semaphore_wait(barrier, nb - 1)
-
-    def points(ref, owner):
-        return ref.at[:, :, pl.ds(pl.multiple_of(owner * width, 128), width)]
-
-    def copy(target, source):
-        return pltpu.make_async_remote_copy(
-            src_ref=ready.at[target],
-            dst_ref=points(out_ref, b),
-            send_sem=sems.at[0, target],
-            recv_sem=sems.at[1, source],
-            device_id={"band": target},
-            device_id_type=MESH,
-        )
-
-    def body(k):
-        at = pl.multiple_of(k * BLOCK, BLOCK)
-        rows = pl.ds(at, BLOCK)
-        inverse = block_inverse(work[rows, pl.ds(at, BLOCK)])
-        final = dot(inverse, rest[rows, :])
-        solved = dot(final, spread_ref[...])
-        for part in range(BLOCK // held):
-            target = k * (BLOCK // held) + part
-            for layer in range(depth):
-                ready[target, layer] = solved[
-                    part * held : (part + 1) * held, layer * width : (layer + 1) * width
-                ]
-
-            @pl.when(target != b)
-            def _():
-                copy(target, b).start()
-
-        upper = dot(inverse, work[rows, :])
-        work[...] -= dot(upper, upper, over_rows)
-        rest[...] -= dot(upper, final, over_rows)
-
-    repeat(size // BLOCK, body)
-    own = pltpu.make_async_copy(ready.at[b], points(out_ref, b), local_sem)
-    own.start()
-    own.wait()
-
-    @functools.partial(repeat, nb - 1)
-    def _(step):
-        copy(band_peer(step), band_peer(step)).wait()
-
-
-def solved_basis(gram, spread, shape, scale):
-    depth, held, cells = shape
-    nb = lax.axis_size("band")
-    size = spread.shape[0]
-    vmem = pl.BlockSpec(memory_space=pltpu.VMEM)
-    return pl.pallas_call(
-        functools.partial(solve_kernel, scale),
-        out_shape=jax.ShapeDtypeStruct(shape, jnp.float32),
-        in_specs=[vmem, vmem],
-        out_specs=pl.BlockSpec(memory_space=pl.ANY),
-        scratch_shapes=[
-            pltpu.VMEM((size, size), jnp.float32),
-            pltpu.VMEM((size, size), jnp.float32),
-            pltpu.VMEM((nb, depth, held, cells // nb), jnp.float32),
-            pltpu.SemaphoreType.DMA((2, nb)),
-            pltpu.SemaphoreType.DMA,
-        ],
-        compiler_params=pltpu.CompilerParams(
-            collective_id=1, has_side_effects=True, vmem_limit_bytes=48 * 1024 * 1024
-        ),
-        name="factor_solve",
-    )(gram, spread)
 
 
 def shards(psi, potential):
@@ -686,16 +682,15 @@
     aligned = (
         bands % (nd * GROUP) == 0
         and cells % (nb * 128) == 0
-        and BLOCK % bands == 0
+        and BLOCK == bands
+        and nd % 2 == 0
+        and depth * nd % 2 == 0
         and bands * nb == GROUP * nd * nb * 2
         and bands * nb == 4 * BLOCK
     )
     if not aligned:
         return staged(psi, potential)
-    spread, gram = spread_and_gram(psi.transpose(1, 0, 2), potential)
-    scale = 1.0 / (depth * nd * cells)
-    out = solved_basis(gram, spread, (depth, bands, cells), scale)
-    return out.transpose(1, 0, 2)
+    return whole(psi.transpose(1, 0, 2), potential).transpose(1, 0, 2)
 
 
 def staged(psi, potential):

time: 160 us -> 146 us (0.912)
  Pallas kernels: 156 us -> 143 us
    pallas_call x2 -> x1, Pallas kernels: 156 us -> 143 us  [whole(): pl.pallas_call(functools.partial(whole_kernel, mine), out_shape=jax.Shape...]
    unnamed x5 -> x1, local copies, waits for them, and re-layouts: 3.63 us -> 2.76 us
where the time goes in v3:
time: 146 us; the launch traced here: 145 us
  Pallas kernels  143 us (98%)
  local copies, waits for them, and re-layouts  2.76 us (2%)
    pallas_call x1, Pallas kernels, whole(): pl.pallas_call(functools.partial(whole_kernel, mine), out_shape=jax.Shape...  143 us

profile of v3, /device:TPU:25, one launch (start us, length us, event | category | flops | bytes accessed | tf_op | source)
XLA Modules:
  0.0 145.4 jit_solution(12991361984936931745)
XLA Ops:
  0.0 142.6 %filter_factor_solve.1 = f32[6,128,512]{2,1,0:T(8,128)} custom-call(f32[6,128,512]{2,1,0:T(8,128)} %bitcast.3, f32[6,512]{1,0:T(8,128)} %pot_ref.1, f32[512,512]{1,0:T(8,128)} %constant.2.clone.plane_ref), custom_call_target="tpu_custom_call" | custom-call | tf_op jit(solution)/shard_map/filter_factor_solve/pallas_call | solution.py:640
  142.6 2.8 %copy.5 = f32[128,6,512]{2,0,1:T(8,128)} copy(f32[128,6,512]{2,0,1:T(8,128)} %bitcast.2) | data formatting | bytes 3145728

commit v4 on v3

--- a/solution.py
+++ b/solution.py
@@ -349,6 +349,17 @@
     )(gram)
 
 
+def split(values):
+    high = values.astype(jnp.bfloat16)
+    return high, (values - high.astype(jnp.float32)).astype(jnp.bfloat16)
+
+
+def split_dot(values, stacked):
+    high, low = split(values)
+    parts = jnp.concatenate([high, low, high], axis=1)
+    return jnp.dot(parts, stacked, preferred_element_type=jnp.float32)
+
+
 def upper_layout(size):
     count = size // BLOCK
     half = count // 2
@@ -376,9 +387,9 @@
 
 
 def whole_kernel(
-    mine, psi_ref, pot_ref, plane_ref, out_ref,
+    mine, psi_ref, pot_ref, stencil_ref, out_ref,
     one, two, diagonal, pots, sent, landed, dom_in, dom_sum, band_in, own, partial,
-    spread_ref, gram_ref, work, rest, inverses, ready, arrived, placed,
+    spread_ref, gram_ref, work, rest, inverses, ready, arrived, placed, matrix, plane_ref,
     dom_sems, pot_sems, all_sems, sum_sems, solve_sems, local_sems,
 ):
     depth, _, cells = psi_ref.shape
@@ -439,6 +450,8 @@
         )
 
     repeat(nd - 1, lambda step: potential_copy(step).start())
+    stencil = pltpu.make_async_copy(stencil_ref, matrix, local_sems.at[1 + halves])
+    stencil.start()
     local = [pltpu.make_async_copy(pot_ref, pots.at[d], local_sems.at[0])]
     for h in range(halves):
         repeat(nd - 1, lambda step, h=h: column_copy(h, step).start())
@@ -447,6 +460,11 @@
         copy.start()
     for copy in local:
         copy.wait()
+    stencil.wait()
+    high, low = split(matrix[...])
+    plane_ref[:cells] = high
+    plane_ref[cells : 2 * cells] = high
+    plane_ref[2 * cells :] = low
     repeat(nd - 1, lambda step: potential_copy(step).wait())
     scale = 3.0 * COEF[0] * KINETIC - CENTRE / HALF_WIDTH
     for owner in range(nd):
@@ -463,7 +481,7 @@
             at = i * chunk
             here = current[h, pl.ds(REACH + at, chunk)]
             flat = here.reshape(chunk * GROUP, cells)
-            total = dot(flat, plane_ref[...]).reshape(here.shape)
+            total = split_dot(flat, plane_ref[...]).reshape(here.shape)
             total = total + here * diagonal[pl.ds(at, chunk)]
             for k in range(1, REACH + 1):
                 above = current[h, pl.ds(REACH + at + k, chunk)]
@@ -634,13 +652,14 @@
     columns = bands + BLOCK
     f32 = jnp.float32
     vmem, where = pl.BlockSpec(memory_space=pltpu.VMEM), pl.BlockSpec(memory_space=pl.ANY)
+    hbm = pl.BlockSpec(memory_space=pl.ANY)
     padded = pltpu.VMEM((halves, layers + 2 * REACH, GROUP, cells), f32)
     piece = (GROUP, columns)
     dma = pltpu.SemaphoreType.DMA
     return pl.pallas_call(
         functools.partial(whole_kernel, mine),
         out_shape=jax.ShapeDtypeStruct(psi.shape, f32),
-        in_specs=[where, vmem, vmem],
+        in_specs=[hbm, vmem, hbm],
         out_specs=where,
         scratch_shapes=[
             padded,
@@ -662,12 +681,14 @@
             pltpu.VMEM((nb, BLOCK, points), f32),
             pltpu.VMEM((nb, BLOCK, points), f32),
             pltpu.VMEM((nb, depth, BLOCK, width), f32),
+            pltpu.VMEM((cells, cells), f32),
+            pltpu.VMEM((3 * cells, cells), jnp.bfloat16),
             dma((2, halves, nd - 1)),
             dma((2, nd - 1)),
             dma((2, halves, total - 1)),
             dma((2, 2 * (nd + nb))),
             dma((2, nb)),
-            dma((max(1 + halves, nb),)),
+            dma((max(2 + halves, nb),)),
         ],
         compiler_params=pltpu.CompilerParams(
             collective_id=0, has_side_effects=True, vmem_limit_bytes=56 * 1024 * 1024

time: 146 us -> 142 us (0.973)
  Pallas kernels: 143 us -> 139 us
    pallas_call x1, Pallas kernels: 143 us -> 139 us  [whole(): pl.pallas_call(functools.partial(whole_kernel, mine), out_shape=jax.Shape...]
where the time goes in v4:
time: 142 us
  Pallas kernels  139 us (98%)
  local copies, waits for them, and re-layouts  2.76 us (2%)
    pallas_call x1, Pallas kernels, whole(): pl.pallas_call(functools.partial(whole_kernel, mine), out_shape=jax.Shape...  139 us

profile of v4, /device:TPU:25, one launch (start us, length us, event | category | flops | bytes accessed | tf_op | source)
XLA Modules:
  0.0 141.8 jit_solution(8388387403622711202)
XLA Ops:
  0.0 139.1 %filter_factor_solve.1 = f32[6,128,512]{2,1,0:T(8,128)} custom-call(f32[6,128,512]{2,1,0:T(8,128)} %bitcast.3, f32[6,512]{1,0:T(8,128)} %pot_ref.1, f32[512,512]{1,0:T(8,128)} %constant.2.clone.stencil_ref), custom_call_target="tpu_custom_call" | custom-call | tf_op jit(solution)/shard_map/filter_factor_solve/pallas_call | solution.py:659
  139.1 2.8 %copy.5 = f32[128,6,512]{2,0,1:T(8,128)} copy(f32[128,6,512]{2,0,1:T(8,128)} %bitcast.2) | data formatting | bytes 3145728
